TPU v7x, 512 devices: a whole 4x4x16 slice. The times are simulated.
512 devices in a mesh: tri: 64 (over y, z), sub: 8 (over x, core).
Axes of the slice: x: 4, y: 4, z: 16, core: 2. Of those that a mesh axis runs over, the one named last changes fastest.
Arguments:
- stored_tiles: float32 [64, 10, 512, 512], P('tri', None, 'sub'), may hold values from -190 to 190, as said below
- cell_owner: int32 [64], replicated, may hold values from 0 to 63, as said below
Outputs:
- updated: float32 [64, 10, 512, 512], P('tri', None, 'sub')
Inputs may be any that keep to these rules, and one draw needn't show every extreme that they name: `cell_owner`: a permutation of the indices of tri. `stored_tiles`: every tile whose row and column blocks are equal is skew-symmetric, every pivot met is invertible, and slots that hold no tile are zero.
All inputs are finite; a program needn't handle non-finite values.
Results may differ from a plain program's by a relative error of at most 0.00035.
Values may be sent and summed in bfloat16 or wider, within the bound.
A program may use at most 64 MiB of HBM per device.

v0:
```python
import math
import jax
import jax.numpy as jnp
import numpy as np
from jax import lax
from jax.sharding import Mesh
from jax.sharding import PartitionSpec as P

NB = 32
TRI = ("tri_0", "tri_1")


def in_order(tiles, dim):
    tiles = jnp.moveaxis(tiles, 0, dim)
    dims = tiles.shape
    return tiles.reshape(*dims[:dim], dims[dim] * dims[dim + 1], *dims[dim + 2 :])


def gather_in_order(x, axes, turns):
    tiles = x[None]
    for k in turns:
        tiles = lax.all_gather(tiles, axes[k], axis=0, tiled=True)
    block = [lax.axis_size(axes[k]) for k in reversed(turns)]
    tiles = tiles.reshape(*block, *x.shape)
    turned = sorted(range(len(turns)), key=lambda place: turns[len(turns) - 1 - place])
    return tiles.transpose(*turned, *range(len(turns), tiles.ndim)).reshape(-1, *x.shape)


def gather_axes(x, axes, turns, dim):
    return in_order(gather_in_order(x, axes, turns), dim)


def layout(groups, per_group):
    half_group = per_group // 2
    slot_count = per_group * (per_group + 1) // 2
    row_table = np.full((groups * groups, slot_count), -1, np.int32)
    col_table = np.full((groups * groups, slot_count), -1, np.int32)
    for first_group in range(groups):
        for second_group in range(groups):
            cell_index = first_group * groups + second_group
            for inner_row in range(per_group):
                if first_group == second_group:
                    for inner_column in range(inner_row + 1):
                        slot_index = inner_row * (inner_row + 1) // 2 + inner_column
                        row_table[cell_index, slot_index] = first_group * per_group + inner_row
                        col_table[cell_index, slot_index] = first_group * per_group + inner_column
                else:
                    for inner_column in range(half_group):
                        slot_index = inner_row * half_group + inner_column
                        if first_group > second_group:
                            row_table[cell_index, slot_index] = first_group * per_group + inner_row
                            col_table[cell_index, slot_index] = (
                                second_group * per_group + inner_column
                            )
                        else:
                            row_table[cell_index, slot_index] = second_group * per_group + inner_row
                            col_table[cell_index, slot_index] = (
                                first_group * per_group + half_group + inner_column
                            )
    return (row_table, col_table)


def shards(stored_tiles, cell_owner):
    tri_count = lax.axis_size(TRI)
    groups = math.isqrt(tri_count)
    per_group = NB // groups
    half_group = per_group // 2
    strip_rows = stored_tiles.shape[2]
    block_order = stored_tiles.shape[3]
    row_table, col_table = layout(groups, per_group)
    position = lax.axis_index(TRI)
    my_cell = jnp.sum(jnp.where(cell_owner == position, jnp.arange(tri_count, dtype=jnp.int32), 0))
    cell_down = my_cell // groups
    cell_across = my_cell % groups
    row_group = jnp.maximum(cell_down, cell_across)
    col_group = jnp.minimum(cell_down, cell_across)
    my_rows = jnp.asarray(row_table)[my_cell]
    my_cols = jnp.asarray(col_table)[my_cell]
    row_local = jnp.clip(my_rows - row_group * per_group, 0, per_group - 1)
    col_local = jnp.clip(my_cols - col_group * per_group, 0, per_group - 1)
    holders = cell_owner[jnp.arange(groups) * groups]
    highest = lax.Precision.HIGHEST
    current = stored_tiles[0]
    lower_slots = np.array([member * half_group for member in range(per_group)], np.int32)
    first_slots = np.array(
        [member * (member + 1) // 2 if member > 0 else 0 for member in range(per_group)], np.int32
    )
    keep_first = np.array([1.0 if member > 0 else 0.0 for member in range(per_group)], np.float32)
    from_lower = current[lower_slots]
    from_first = current[first_slots] * keep_first[:, None, None]
    holder_part = jnp.where(cell_down > 0, from_lower, from_first)
    holder_part = jnp.where(cell_across == 0, holder_part, 0.0).astype(jnp.bfloat16)
    pivot_slot = 0 // 2
    pivot_part = jnp.where(my_cell == 0, current[pivot_slot], 0.0)
    piece_size = holder_part.size // tri_count
    spread_panel = lax.all_to_all(
        holder_part.reshape(tri_count, piece_size), TRI, split_axis=0, concat_axis=0, tiled=True
    )
    spread_pivot = lax.all_to_all(
        pivot_part.astype(jnp.bfloat16), TRI, split_axis=0, concat_axis=0, tiled=True
    ).astype(pivot_part.dtype)
    picked_panel = spread_panel[holders][:, None, :]
    picked_pivot = spread_pivot[holders[0]][None, :]
    whole_panel = gather_axes(picked_panel, TRI, (0, 1), 1)
    whole_pivot = gather_axes(picked_pivot.astype(jnp.bfloat16), TRI, (0, 1), 0).astype(
        picked_pivot.dtype
    )
    panels = whole_panel.reshape(groups, per_group, strip_rows, block_order)
    own_strips = panels[row_group]
    other_strips = panels[col_group]
    pivot_block = lax.all_gather(
        whole_pivot.astype(jnp.bfloat16), "sub", axis=0, tiled=True
    ).astype(whole_pivot.dtype)
    partner = lax.all_gather(other_strips, "sub", axis=1, tiled=True)
    gram_matrix = jnp.dot(pivot_block.T, pivot_block, precision=highest)
    factor = jnp.linalg.cholesky(gram_matrix)
    inverse = jax.scipy.linalg.cho_solve((factor, True), pivot_block.T)
    scaled = jnp.einsum(
        "irk,kc->irc", own_strips.astype(jnp.float32), inverse, precision=highest
    ).astype(jnp.bfloat16)
    left_slots = scaled[row_local]
    right_slots = partner[col_local]
    update = jnp.einsum("qrk,qck->qrc", left_slots, right_slots, preferred_element_type=jnp.float32)
    live_slots = (my_rows > 0) & (my_cols > 0)
    current = current + jnp.where(live_slots[:, None, None], update, 0.0)
    return current[None]


def solution(mesh):
    torus = Mesh(mesh.devices.reshape(4, 16, mesh.shape["sub"]), ("tri_0", "tri_1", "sub"))
    return jax.shard_map(
        shards,
        mesh=torus,
        in_specs=(P(TRI, None, "sub", None), P()),
        out_specs=P(TRI, None, "sub", None),
        check_vma=False,
    )
```

profile of v0, /device:TPU:1, one launch (start us, length us, event | category | flops | bytes accessed | tf_op | source)
XLA Modules:
  0.0 323.7 jit_solution(5538113034983923474)
XLA Ops:
  6.5 1.4 fusion.56
  11.3 19.3 %all-to-all-start.1 = ((bf16[64,2,256]{2,1,0:T(2,128)(2,1)}), bf16[64,2,256]{2,1,0:T(2,128)(2,1)S(1)}, u32[]{:S(2)}, u32[]{:S(2)}) async-start(bf16[64,2,256]{2,1,0:T(2,128)(2,1)} %reshape.305), calls=%async_computation.1 | async-start | bytes 131072 | tf_op jit(solution)/shard_map/all_to_all | solution.py:99
  33.4 1.3 gather_fusion.2
  35.4 1.9 gather_fusion.1
  37.3 1.9 gather_fusion
  43.2 2.1 reduce.26
  46.2 14.6 %all-to-all-start = ((bf16[64,2,1024]{2,1,0:T(2,128)(2,1)}), bf16[64,2,1024]{2,1,0:T(2,128)(2,1)S(1)}, u32[]{:S(2)}, u32[]{:S(2)}) async-start(bf16[64,2,1024]{2,1,0:T(2,128)(2,1)} %reshape.307), calls=%async_computation | async-start | bytes 524288 | tf_op jit(solution)/shard_map/all_to_all | solution.py:96
  60.9 8.8 %all_gather.20 = bf16[4,1,512]{2,1,0:T(2,128)(2,1)S(1)} all-gather(bf16[1,1,512]{2,1,0:T(2,128)(2,1)S(1)} %fusion.54), channel_id=1, replica_groups=mesh['tri_0'=4,'tri_1'=16,'sub'=8] {'tri_0'}, dimensions={0}, use_global_device_ids=true | all-gather | bytes 5120 | tf_op jit(solution)/shard_map/all_gather | solution.py:22
  69.7 23.8 %all_gather.21 = bf16[64,1,512]{2,1,0:T(2,128)(2,1)S(1)} all-gather(bf16[4,1,512]{2,1,0:T(2,128)(2,1)S(1)} %all_gather.20), channel_id=1, replica_groups=mesh['tri_0'=4,'tri_1'=16,'sub'=8] {'tri_1'}, dimensions={0}, use_global_device_ids=true | all-gather | bytes 69632 | tf_op jit(solution)/shard_map/all_gather | solution.py:22
  93.9 23.9 %all_gather.22 = bf16[512,512]{1,0:T(8,128)(2,1)S(1)} all-gather(bf16[64,512]{1,0:T(8,128)(2,1)S(1)} %bitcast.120), channel_id=1, replica_groups=mesh['tri_0'=4,'tri_1'=16,'sub'=8] {'sub'}, dimensions={0}, use_global_device_ids=true | all-gather | bytes 589824 | tf_op jit(solution)/shard_map/all_gather | solution.py:111
  119.9 11.7 %cholesky.104 = f32[128,128]{1,0:T(8,128)S(1)} custom-call(f32[128,128]{1,0:T(8,128)S(1)} %cholesky.266), custom_call_target="Cholesky" | custom-call | tf_op jit(solution)/shard_map/jit(cholesky)/cholesky | solution.py:116
  131.6 9.8 %custom-call.34 = f32[1,128,128]{1,2,0:T(8,128)S(1)} custom-call(f32[1,128,128]{2,1,0:T(8,128)S(1)} %get-tuple-element.32), custom_call_target="InvertDiagBlocksLowerTriangular" | custom-call | tf_op jit(solution)/shard_map/jit(cholesky)/cholesky | solution.py:116
  142.6 9.8 %all-gather = bf16[32,2048]{1,0:T(8,128)(2,1)} all-gather(bf16[8,2048]{1,0:T(8,128)(2,1)S(1)} %gather_fusion.3), channel_id=2, replica_groups=mesh['tri_0'=4,'tri_1'=16,'sub'=8] {'tri_0'}, dimensions={0}, use_global_device_ids=true | all-gather | bytes 163840 | tf_op jit(solution)/shard_map/all_gather | solution.py:22
  154.3 11.7 %cholesky.217 = f32[128,128]{1,0:T(8,128)S(1)} custom-call(f32[128,128]{1,0:T(8,128)S(1)} %cholesky.270), custom_call_target="Cholesky" | custom-call | tf_op jit(solution)/shard_map/jit(cholesky)/cholesky | solution.py:116
  166.1 9.8 %custom-call.35 = f32[1,128,128]{1,2,0:T(8,128)S(1)} custom-call(f32[1,128,128]{2,1,0:T(8,128)S(1)} %get-tuple-element.29), custom_call_target="InvertDiagBlocksLowerTriangular" | custom-call | tf_op jit(solution)/shard_map/jit(cholesky)/cholesky | solution.py:116
  176.6 11.7 %cholesky.238 = f32[128,128]{1,0:T(8,128)S(1)} custom-call(f32[128,128]{1,0:T(8,128)S(1)} %cholesky.275), custom_call_target="Cholesky" | custom-call | tf_op jit(solution)/shard_map/jit(cholesky)/cholesky | solution.py:116
  188.3 10.0 %custom-call.36 = f32[1,128,128]{1,2,0:T(8,128)S(1)} custom-call(f32[1,128,128]{2,1,0:T(8,128)S(1)} %get-tuple-element.26), custom_call_target="InvertDiagBlocksLowerTriangular" | custom-call | tf_op jit(solution)/shard_map/jit(cholesky)/cholesky | solution.py:116
  198.9 11.7 %cholesky.255 = f32[128,128]{1,0:T(8,128)S(1)} custom-call(f32[128,128]{1,0:T(8,128)S(1)} %convolution_subtract_fusion.8), custom_call_target="Cholesky" | custom-call | tf_op jit(solution)/shard_map/jit(cholesky)/cholesky | solution.py:116
  215.7 10.8 %while.1 = (s32[]{:T(128)}, f32[512,512]{1,0:T(8,128)S(1)}, s32[4,2]{0,1:T(2,128)S(1)}, f32[4,128,128]{2,1,0:T(8,128)}, s32[]{:T(128)}) while((s32[]{:T(128)}, f32[512,512]{1,0:T(8,128)S(1)}, s32[4,2]{0,1:T(2,128)S(1)}, f32[4,128,128]{2,1,0:T(8,128)}, s32[]{:T(128)}) %tuple.27), condition=%wide.while_cond, body=%wide.while_body.sunk | while | flops 2 | bytes 132705 | solution.py:117
  216.4 2.0 bitcast_dynamic-update-slice_fusion.2
  219.1 2.0 bitcast_dynamic-update-slice_fusion.2
  221.8 2.0 bitcast_dynamic-update-slice_fusion.2
  224.5 2.0 bitcast_dynamic-update-slice_fusion.2
  226.5 40.1 %custom-call.37 = f32[4,128,128]{1,2,0:T(8,128)S(1)} custom-call(f32[4,128,128]{2,1,0:T(8,128)} %get-tuple-element.12), custom_call_target="InvertDiagBlocksLowerTriangular" | custom-call | tf_op jit(solution)/shard_map/jit(_cho_solve)/triangular_solve | solution.py:117
  266.7 1.7 copy.27
  269.6 2.6 reshape_reshape.6
  272.2 1.7 constant_dynamic-slice_fusion.1
  273.9 1.2 fusion.35
  282.1 1.6 convolution_convert_fusion
  284.3 21.5 %all-gather.7.cloned.1.call-done = bf16[1,4,512,512]{3,2,1,0:T(8,128)(2,1)} async-done(((bf16[1,4,64,512]{3,2,1,0:T(8,128)(2,1)}), bf16[1,4,512,512]{3,2,1,0:T(8,128)(2,1)}) %all-gather.7.cloned.1.call-update) | async-done | bytes 2097168 | tf_op jit(solution)/shard_map/all_gather | solution.py:114
  305.8 5.5 %gather_fusion.5 = bf16[10,512,512]{2,1,0:T(8,128)(2,1)} fusion(bf16[4,512,512]{2,1,0:T(8,128)(2,1)} %bitcast.112, s32[1024]{0:T(1024)S(1)} %pad_clamp_fusion), kind=kCustom, calls=%fused_computation.5 | custom fusion | bytes 10485800 | tf_op jit(solution)/shard_map/gather | solution.py:122
  311.4 5.2 %fusion.1 = f32[1,10,64,512]{3,2,1,0:T(8,128)} fusion(bf16[10,64,512]{2,1,0:T(8,128)(2,1)S(1)} %gather_fusion.4, bf16[10,512,512]{2,1,0:T(8,128)(2,1)} %gather_fusion.5, pred[10]{0:T(512)(128)(4,1)S(1)} %and_bitcast_fusion, f32[1,10,64,512]{3,2,1,0:T(8,128)S(1)} %copy-done), kind=kOutput, calls=%fused_computation.10 | convolution fusion | flops 336199680 | bytes 8519690 | tf_op jit(solution)/shard_map/qrk,qck->qrc/dot_general | solution.py:123
  (91 shorter events, 27.2 us)
Async XLA Ops:
  6.5 35.5 %copy-start.3 = (f32[4]{0:T(128)S(1)}, f32[4]{0:T(128)}, u32[]{:S(2)}) copy-start(f32[4]{0:T(128)} %constant.245) | copy-start | bytes 52
  11.3 34.9 %all-to-all-start.1 = ((bf16[64,2,256]{2,1,0:T(2,128)(2,1)}), bf16[64,2,256]{2,1,0:T(2,128)(2,1)S(1)}, u32[]{:S(2)}, u32[]{:S(2)}) async-start(bf16[64,2,256]{2,1,0:T(2,128)(2,1)} %reshape.305), calls=%async_computation.1 | async-start | bytes 131072 | tf_op jit(solution)/shard_map/all_to_all | solution.py:99
  46.2 95.4 %all-to-all-start = ((bf16[64,2,1024]{2,1,0:T(2,128)(2,1)}), bf16[64,2,1024]{2,1,0:T(2,128)(2,1)S(1)}, u32[]{:S(2)}, u32[]{:S(2)}) async-start(bf16[64,2,1024]{2,1,0:T(2,128)(2,1)} %reshape.307), calls=%async_computation | async-start | bytes 524288 | tf_op jit(solution)/shard_map/all_to_all | solution.py:96
  60.8 205.9 %all-gather.5.cloned.1.call-start = ((), (), s32[]{:S(2)}) async-start(), calls=%async_computation.2 | async-start | bytes 2228224 | tf_op jit(solution)/shard_map/all_gather | solution.py:22
  118.9 1.0 copy-start.1
  119.9 32.8 %copy-start.2 = (f32[512,512]{1,0:T(8,128)S(1)}, f32[512,512]{1,0:T(8,128)}, u32[]{:S(2)}) copy-start(f32[512,512]{1,0:T(8,128)} %copy-done.1) | copy-start | bytes 3145732
  152.4 153.4 %all-gather.7.cloned.1.call-start = ((), (), s32[]{:S(2)}) async-start(), calls=%async_computation.3 | async-start | bytes 2359296 | tf_op jit(solution)/shard_map/all_gather | solution.py:114
  305.8 5.6 %copy-start = (f32[1,10,64,512]{3,2,1,0:T(8,128)S(1)}, f32[1,10,64,512]{3,2,1,0:T(8,128)}, u32[]{:S(2)}) copy-start(f32[1,10,64,512]{3,2,1,0:T(8,128)} %param.9) | copy-start | bytes 3932164
Sparse Core Ops, SparseCore 0:
  152.6 63.2 all-gather.4
  274.0 31.7 all-gather.6
where the time goes:
time: 329 us; the launch traced here: 324 us
  other arithmetic  129 us (39%)
  blocking collectives  66.3 us (20%)
  local copies, waits for them, and re-layouts  34.9 us (11%)
  starting transfers between devices  34.1 us (10%)
  between operations  21.9 us (7%)
  waiting for transfers between devices  21.6 us (7%)
  matrix products  16.1 us (5%)
    another operation x14, other arithmetic, shards(): factor = jnp.linalg.cholesky(gram_matrix)  78.8 us
    all_gather x3, blocking collectives, gather_in_order(): tiles = lax.all_gather(tiles, axes[k], axis=0, tiled=True)  42.5 us
    another operation x3, other arithmetic, shards(): inverse = jax.scipy.linalg.cho_solve((factor, True), pivot_block.T)  40.3 us
    all_gather x1, blocking collectives, shards(): lax.all_gather(whole_pivot.astype(jnp.bfloat16), 'sub', axis=0, tiled=True)  23.9 us
    all_gather x1, waiting for transfers between devices, shards(): partner = lax.all_gather(other_strips, 'sub', axis=1, tiled=True)  21.5 us
    all_to_all x1, starting transfers between devices, shards(): lax.all_to_all(pivot_part.astype(jnp.bfloat16), TRI, split_axis=0, concat...  19.3 us
    all_to_all x1, starting transfers between devices, shards(): lax.all_to_all(holder_part.reshape(tri_count, piece_size), TRI, split_axi...  14.6 us
    another operation x12, local copies, waits for them, and re-layouts  10.8 us
  transfers between devices with their start and end apart: 4, of which 1 were waited for; matrix products, arithmetic and copies ran while one was open for 48% of the time, Pallas kernels for 0%

commit v1 on v0

--- a/solution.py
+++ b/solution.py
@@ -8,6 +8,27 @@
 
 NB = 32
 TRI = ("tri_0", "tri_1")
+
+
+def joined_along(tiles, dim):
+    tiles = jnp.moveaxis(tiles, 0, dim)
+    lengths = tiles.shape
+    return tiles.reshape(*lengths[:dim], lengths[dim] * lengths[dim + 1], *lengths[dim + 2 :])
+
+
+def grow_blocks(shard, axis):
+    size, place = (lax.axis_size(axis), lax.axis_index(axis))
+    blocks, distance = (shard[None], 1)
+    while distance < size:
+        other = lax.ppermute(blocks, axis, [(i, i ^ distance) for i in range(size)])
+        low = place & distance == 0
+        blocks = jnp.concatenate([jnp.where(low, blocks, other), jnp.where(low, other, blocks)])
+        distance *= 2
+    return blocks
+
+
+def gather_by_bits(array, axis, dim):
+    return joined_along(grow_blocks(array, axis), dim)
 
 
 def in_order(tiles, dim):
@@ -108,9 +129,9 @@
     panels = whole_panel.reshape(groups, per_group, strip_rows, block_order)
     own_strips = panels[row_group]
     other_strips = panels[col_group]
-    pivot_block = lax.all_gather(
-        whole_pivot.astype(jnp.bfloat16), "sub", axis=0, tiled=True
-    ).astype(whole_pivot.dtype)
+    pivot_block = gather_by_bits(whole_pivot.astype(jnp.bfloat16), "sub", 0).astype(
+        whole_pivot.dtype
+    )
     partner = lax.all_gather(other_strips, "sub", axis=1, tiled=True)
     gram_matrix = jnp.dot(pivot_block.T, pivot_block, precision=highest)
     factor = jnp.linalg.cholesky(gram_matrix)

time: 329 us -> 334 us (1.015)
  blocking collectives: 66.3 us -> 42.8 us
  starting transfers between devices: 34.1 us -> 54.1 us
  waiting for transfers between devices: 21.6 us -> 31.3 us
    all_gather x1 -> x0, blocking collectives: 23.9 us -> none  [shards(): lax.all_gather(whole_pivot.astype(jnp.bfloat16), 'sub', axis=0, tiled=True)]
    ppermute x0 -> x3, starting transfers between devices: none -> 20.3 us  [grow_blocks(): other = lax.ppermute(blocks, axis, [(i, i ^ distance) for i in range(size)])]
    ppermute x0 -> x3, waiting for transfers between devices: none -> 7.1 us  [grow_blocks(): other = lax.ppermute(blocks, axis, [(i, i ^ distance) for i in range(size)])]
  transfers between devices with their start and end apart: 4 -> 7, of which waited for: 1 -> 5; matrix products, arithmetic and copies ran while one was open for 48% -> 47% of each run, Pallas kernels for 0% -> 0%
where the time goes in v1:
time: 334 us; the launch traced here: 328 us
  other arithmetic  129 us (39%)
  starting transfers between devices  54.1 us (16%)
  blocking collectives  42.8 us (13%)
  local copies, waits for them, and re-layouts  34.1 us (10%)
  waiting for transfers between devices  31.3 us (9%)
  between operations  21.2 us (6%)
  matrix products  16.1 us (5%)
    another operation x14, other arithmetic, shards(): factor = jnp.linalg.cholesky(gram_matrix)  78.6 us
    all_gather x3, blocking collectives, gather_in_order(): tiles = lax.all_gather(tiles, axes[k], axis=0, tiled=True)  42.8 us
    another operation x3, other arithmetic, shards(): inverse = jax.scipy.linalg.cho_solve((factor, True), pivot_block.T)  40.3 us
    all_gather x1, waiting for transfers between devices, shards(): partner = lax.all_gather(other_strips, 'sub', axis=1, tiled=True)  23.8 us
    ppermute x3, starting transfers between devices, grow_blocks(): other = lax.ppermute(blocks, axis, [(i, i ^ distance) for i in range(size)])  20.3 us
    all_to_all x1, starting transfers between devices, shards(): lax.all_to_all(pivot_part.astype(jnp.bfloat16), TRI, split_axis=0, concat...  19.3 us
    all_to_all x1, starting transfers between devices, shards(): lax.all_to_all(holder_part.reshape(tri_count, piece_size), TRI, split_axi...  14.2 us
    another operation x12, local copies, waits for them, and re-layouts  10.6 us
  transfers between devices with their start and end apart: 7, of which 5 were waited for; matrix products, arithmetic and copies ran while one was open for 47% of the time, Pallas kernels for 0%

profile of v1, /device:TPU:1, one launch (start us, length us, event | category | flops | bytes accessed | tf_op | source)
XLA Modules:
  0.0 328.5 jit_solution(12710778907257383376)
XLA Ops:
  11.4 19.3 %all-to-all-start.1 = ((bf16[64,2,256]{2,1,0:T(2,128)(2,1)}), bf16[64,2,256]{2,1,0:T(2,128)(2,1)S(1)}, u32[]{:S(2)}, u32[]{:S(2)}) async-start(bf16[64,2,256]{2,1,0:T(2,128)(2,1)} %reshape.311), calls=%async_computation.1 | async-start | bytes 131072 | tf_op jit(solution)/shard_map/all_to_all | solution.py:120
  35.9 1.9 gather_fusion.1
  37.9 1.9 gather_fusion
  40.1 2.2 reduce.26
  44.2 14.2 %all-to-all-start = ((bf16[64,2,1024]{2,1,0:T(2,128)(2,1)}), bf16[64,2,1024]{2,1,0:T(2,128)(2,1)S(1)}, u32[]{:S(2)}, u32[]{:S(2)}) async-start(bf16[64,2,1024]{2,1,0:T(2,128)(2,1)} %reshape.313), calls=%async_computation | async-start | bytes 524288 | tf_op jit(solution)/shard_map/all_to_all | solution.py:117
  58.6 8.8 %all_gather.17 = bf16[4,1,512]{2,1,0:T(2,128)(2,1)S(1)} all-gather(bf16[1,1,512]{2,1,0:T(2,128)(2,1)S(1)} %fusion.54), channel_id=1, replica_groups=mesh['tri_0'=4,'tri_1'=16,'sub'=8] {'tri_0'}, dimensions={0}, use_global_device_ids=true | all-gather | bytes 5120 | tf_op jit(solution)/shard_map/all_gather | solution.py:43
  67.4 23.8 %all_gather.18 = bf16[64,1,512]{2,1,0:T(2,128)(2,1)S(1)} all-gather(bf16[4,1,512]{2,1,0:T(2,128)(2,1)S(1)} %all_gather.17), channel_id=1, replica_groups=mesh['tri_0'=4,'tri_1'=16,'sub'=8] {'tri_1'}, dimensions={0}, use_global_device_ids=true | all-gather | bytes 69632 | tf_op jit(solution)/shard_map/all_gather | solution.py:43
  91.6 12.0 %collective-permute-start = (bf16[1,64,512]{2,1,0:T(8,128)(2,1)S(1)}, bf16[1,64,512]{2,1,0:T(8,128)(2,1)S(1)}, u32[]{:S(2)}, u32[]{:S(2)}) collective-permute-start(bf16[1,64,512]{2,1,0:T(8,128)(2,1)S(1)} %bitcast.125), channel_id=1, source_target_pairs={{0,1},{1,0},{2,3},{3,2},{4,5},{5,4},{6,7},{7,6},{8,9},{9,8},{10,11... | collective-permute-start | bytes 196616 | tf_op jit(solution)/shard_map/ppermute | solution.py:23
  104.6 3.1 collective-permute-start.1
  108.4 2.8 collective-permute-done.1
  111.3 5.1 %collective-permute-start.2 = (bf16[4,64,512]{2,1,0:T(8,128)(2,1)S(1)}, bf16[4,64,512]{2,1,0:T(8,128)(2,1)S(1)}, u32[]{:S(2)}, u32[]{:S(2)}) collective-permute-start(bf16[4,64,512]{2,1,0:T(8,128)(2,1)S(1)} %pad_maximum_fusion.1), channel_id=1, source_target_pairs={{0,4},{1,5},{2,6},{3,7},{4,0},{5,1},{6,2},{7,3},{8,12},{9,13},{10,... | collective-permute-start | bytes 786440 | tf_op jit(solution)/shard_map/ppermute | solution.py:23
  117.8 3.5 %collective-permute-done.2 = bf16[4,64,512]{2,1,0:T(8,128)(2,1)S(1)} collective-permute-done((bf16[4,64,512]{2,1,0:T(8,128)(2,1)S(1)}, bf16[4,64,512]{2,1,0:T(8,128)(2,1)S(1)}, u32[]{:S(2)}, u32[]{:S(2)}) %collective-permute-start.2) | collective-permute-done | bytes 262176 | tf_op jit(solution)/shard_map/ppermute | solution.py:23
  122.7 11.7 %cholesky.104 = f32[128,128]{1,0:T(8,128)S(1)} custom-call(f32[128,128]{1,0:T(8,128)S(1)} %cholesky.266), custom_call_target="Cholesky" | custom-call | tf_op jit(solution)/shard_map/jit(cholesky)/cholesky | solution.py:137
  134.6 9.8 %custom-call.34 = f32[1,128,128]{1,2,0:T(8,128)S(1)} custom-call(f32[1,128,128]{2,1,0:T(8,128)S(1)} %get-tuple-element.38), custom_call_target="InvertDiagBlocksLowerTriangular" | custom-call | tf_op jit(solution)/shard_map/jit(cholesky)/cholesky | solution.py:137
  145.7 10.1 %all-gather = bf16[32,2048]{1,0:T(8,128)(2,1)} all-gather(bf16[8,2048]{1,0:T(8,128)(2,1)S(1)} %gather_fusion.3), channel_id=2, replica_groups=mesh['tri_0'=4,'tri_1'=16,'sub'=8] {'tri_0'}, dimensions={0}, use_global_device_ids=true | all-gather | bytes 163840 | tf_op jit(solution)/shard_map/all_gather | solution.py:43
  156.5 11.7 %cholesky.217 = f32[128,128]{1,0:T(8,128)S(1)} custom-call(f32[128,128]{1,0:T(8,128)S(1)} %cholesky.270), custom_call_target="Cholesky" | custom-call | tf_op jit(solution)/shard_map/jit(cholesky)/cholesky | solution.py:137
  168.2 9.8 %custom-call.35 = f32[1,128,128]{1,2,0:T(8,128)S(1)} custom-call(f32[1,128,128]{2,1,0:T(8,128)S(1)} %get-tuple-element.35), custom_call_target="InvertDiagBlocksLowerTriangular" | custom-call | tf_op jit(solution)/shard_map/jit(cholesky)/cholesky | solution.py:137
  178.7 11.7 %cholesky.238 = f32[128,128]{1,0:T(8,128)S(1)} custom-call(f32[128,128]{1,0:T(8,128)S(1)} %cholesky.275), custom_call_target="Cholesky" | custom-call | tf_op jit(solution)/shard_map/jit(cholesky)/cholesky | solution.py:137
  190.5 10.0 %custom-call.36 = f32[1,128,128]{1,2,0:T(8,128)S(1)} custom-call(f32[1,128,128]{2,1,0:T(8,128)S(1)} %get-tuple-element.32), custom_call_target="InvertDiagBlocksLowerTriangular" | custom-call | tf_op jit(solution)/shard_map/jit(cholesky)/cholesky | solution.py:137
  201.1 11.7 %cholesky.255 = f32[128,128]{1,0:T(8,128)S(1)} custom-call(f32[128,128]{1,0:T(8,128)S(1)} %convolution_subtract_fusion.8), custom_call_target="Cholesky" | custom-call | tf_op jit(solution)/shard_map/jit(cholesky)/cholesky | solution.py:137
  217.4 10.6 %while.1 = (s32[]{:T(128)}, f32[512,512]{1,0:T(8,128)S(1)}, s32[4,2]{0,1:T(2,128)S(1)}, f32[4,128,128]{2,1,0:T(8,128)}, s32[]{:T(128)}) while((s32[]{:T(128)}, f32[512,512]{1,0:T(8,128)S(1)}, s32[4,2]{0,1:T(2,128)S(1)}, f32[4,128,128]{2,1,0:T(8,128)}, s32[]{:T(128)}) %tuple.30), condition=%wide.while_cond, body=%wide.while_body.sunk | while | flops 2 | bytes 132705 | solution.py:138
  218.1 2.0 bitcast_dynamic-update-slice_fusion.2
  220.7 2.0 bitcast_dynamic-update-slice_fusion.2
  223.4 2.0 bitcast_dynamic-update-slice_fusion.2
  226.0 2.0 bitcast_dynamic-update-slice_fusion.2
  228.0 40.1 %custom-call.37 = f32[4,128,128]{1,2,0:T(8,128)S(1)} custom-call(f32[4,128,128]{2,1,0:T(8,128)} %get-tuple-element.12), custom_call_target="InvertDiagBlocksLowerTriangular" | custom-call | tf_op jit(solution)/shard_map/jit(_cho_solve)/triangular_solve | solution.py:138
  269.2 1.7 copy.29
  272.1 2.6 reshape_reshape.4
  274.7 1.7 constant_dynamic-slice_fusion.1
  286.8 23.8 %all-gather.7.cloned.1.call-done = bf16[1,4,512,512]{3,2,1,0:T(8,128)(2,1)} async-done(((bf16[1,4,64,512]{3,2,1,0:T(8,128)(2,1)}), bf16[1,4,512,512]{3,2,1,0:T(8,128)(2,1)}) %all-gather.7.cloned.1.call-update) | async-done | bytes 2097168 | tf_op jit(solution)/shard_map/all_gather | solution.py:135
  310.6 5.5 %gather_fusion.5 = bf16[10,512,512]{2,1,0:T(8,128)(2,1)} fusion(bf16[4,512,512]{2,1,0:T(8,128)(2,1)} %bitcast.115, s32[1024]{0:T(1024)S(1)} %pad_clamp_fusion), kind=kCustom, calls=%fused_computation.5 | custom fusion | bytes 10485800 | tf_op jit(solution)/shard_map/gather | solution.py:143
  316.2 5.2 %fusion.1 = f32[1,10,64,512]{3,2,1,0:T(8,128)} fusion(bf16[10,64,512]{2,1,0:T(8,128)(2,1)S(1)} %gather_fusion.4, bf16[10,512,512]{2,1,0:T(8,128)(2,1)} %gather_fusion.5, pred[10]{0:T(512)(128)(4,1)S(1)} %and_bitcast_fusion, f32[1,10,64,512]{3,2,1,0:T(8,128)S(1)} %copy-done), kind=kOutput, calls=%fused_computation.10 | convolution fusion | flops 336199680 | bytes 8519690 | tf_op jit(solution)/shard_map/qrk,qck->qrc/dot_general | solution.py:144
  (106 shorter events, 33.5 us)
Async XLA Ops:
  6.5 33.2 %copy-start.5 = (f32[4]{0:T(128)S(1)}, f32[4]{0:T(128)}, u32[]{:S(2)}) copy-start(f32[4]{0:T(128)} %constant.250) | copy-start | bytes 52
  11.4 32.8 %all-to-all-start.1 = ((bf16[64,2,256]{2,1,0:T(2,128)(2,1)}), bf16[64,2,256]{2,1,0:T(2,128)(2,1)S(1)}, u32[]{:S(2)}, u32[]{:S(2)}) async-start(bf16[64,2,256]{2,1,0:T(2,128)(2,1)} %reshape.311), calls=%async_computation.1 | async-start | bytes 131072 | tf_op jit(solution)/shard_map/all_to_all | solution.py:120
  44.2 100.5 %all-to-all-start = ((bf16[64,2,1024]{2,1,0:T(2,128)(2,1)}), bf16[64,2,1024]{2,1,0:T(2,128)(2,1)S(1)}, u32[]{:S(2)}, u32[]{:S(2)}) async-start(bf16[64,2,1024]{2,1,0:T(2,128)(2,1)} %reshape.313), calls=%async_computation | async-start | bytes 524288 | tf_op jit(solution)/shard_map/all_to_all | solution.py:117
  58.5 210.7 %all-gather.5.cloned.1.call-start = ((), (), s32[]{:S(2)}) async-start(), calls=%async_computation.2 | async-start | bytes 2228224 | tf_op jit(solution)/shard_map/all_gather | solution.py:43
  91.6 12.9 %collective-permute-start = (bf16[1,64,512]{2,1,0:T(8,128)(2,1)S(1)}, bf16[1,64,512]{2,1,0:T(8,128)(2,1)S(1)}, u32[]{:S(2)}, u32[]{:S(2)}) collective-permute-start(bf16[1,64,512]{2,1,0:T(8,128)(2,1)S(1)} %bitcast.125), channel_id=1, source_target_pairs={{0,1},{1,0},{2,3},{3,2},{4,5},{5,4},{6,7},{7,6},{8,9},{9,8},{10,11... | collective-permute-start | bytes 196616 | tf_op jit(solution)/shard_map/ppermute | solution.py:23
  104.6 6.6 %collective-permute-start.1 = (bf16[2,64,512]{2,1,0:T(8,128)(2,1)S(1)}, bf16[2,64,512]{2,1,0:T(8,128)(2,1)S(1)}, u32[]{:S(2)}, u32[]{:S(2)}) collective-permute-start(bf16[2,64,512]{2,1,0:T(8,128)(2,1)S(1)} %pad_maximum_fusion.2), channel_id=1, source_target_pairs={{0,2},{1,3},{2,0},{3,1},{4,6},{5,7},{6,4},{7,5},{8,10},{9,11},{10,... | collective-permute-start | bytes 393224 | tf_op jit(solution)/shard_map/ppermute | solution.py:23
  111.3 10.0 %collective-permute-start.2 = (bf16[4,64,512]{2,1,0:T(8,128)(2,1)S(1)}, bf16[4,64,512]{2,1,0:T(8,128)(2,1)S(1)}, u32[]{:S(2)}, u32[]{:S(2)}) collective-permute-start(bf16[4,64,512]{2,1,0:T(8,128)(2,1)S(1)} %pad_maximum_fusion.1), channel_id=1, source_target_pairs={{0,4},{1,5},{2,6},{3,7},{4,0},{5,1},{6,2},{7,3},{8,12},{9,13},{10,... | collective-permute-start | bytes 786440 | tf_op jit(solution)/shard_map/ppermute | solution.py:23
  121.3 0.7 copy-start.1
  121.3 0.8 copy-start.3
  155.9 154.7 %all-gather.7.cloned.1.call-start = ((), (), s32[]{:S(2)}) async-start(), calls=%async_computation.3 | async-start | bytes 2359296 | tf_op jit(solution)/shard_map/all_gather | solution.py:135
  178.7 89.4 %copy-start.2 = (bf16[4,64,512]{2,1,0:T(8,128)(2,1)S(1)}, bf16[4,64,512]{2,1,0:T(8,128)(2,1)}, u32[]{:S(2)}) copy-start(bf16[4,64,512]{2,1,0:T(8,128)(2,1)} %copy-done.1) | copy-start | bytes 786436
  178.7 89.4 %copy-start.4 = (bf16[4,64,512]{2,1,0:T(8,128)(2,1)S(1)}, bf16[4,64,512]{2,1,0:T(8,128)(2,1)}, u32[]{:S(2)}) copy-start(bf16[4,64,512]{2,1,0:T(8,128)(2,1)} %copy-done.3) | copy-start | bytes 786436
  310.6 5.6 %copy-start = (f32[1,10,64,512]{3,2,1,0:T(8,128)S(1)}, f32[1,10,64,512]{3,2,1,0:T(8,128)}, u32[]{:S(2)}) copy-start(f32[1,10,64,512]{3,2,1,0:T(8,128)} %param.9) | copy-start | bytes 3932164
Sparse Core Ops, SparseCore 0:
  156.0 65.5 all-gather.4
  276.5 34.0 all-gather.6
